TPU v7x, 32 devices: a whole 2x2x4 slice. The times are simulated.
32 devices in a mesh: pitch: 4 (over z), radial: 4 (over y, core), axial: 2 (over x).
Axes of the slice: x: 2, y: 2, z: 4, core: 2. Of those that a mesh axis runs over, the one named last changes fastest.
Arguments:
- density: float32 [9, 4, 32, 512], P(None, 'axial', 'radial', 'pitch'), may hold values from 0.5 to 2
- moments: float32 [9, 4, 4, 32, 512], P(None, None, 'axial', 'radial', 'pitch'), may hold values from -6 to 6
- shifts: int32 [9], replicated, may hold values from 0 to 511, as said below
Outputs:
- residual: float32 [9, 5, 4, 32, 512], P(None, None, 'axial', 'radial', 'pitch')
- update: float32 [9, 5, 4, 32, 512], P(None, None, 'axial', 'radial', 'pitch')
Inputs may be any that keep to these rules, and one draw needn't show every extreme that they name: `shifts`: every instance's offset lies in 0 to 511 and some instance has offset 512 - 1.
All inputs are finite; a program needn't handle non-finite values.
Results may differ from a plain program's by a relative error of at most 0.0005.
Values sent between devices are 32-bit elements; how exact they have to be, the bound alone decides.
A program may use at most 192 MiB of HBM per device.

v0:
```python
import math

import jax
import jax.numpy as jnp
import numpy as np
from jax import lax
from jax.sharding import PartitionSpec as P

COEFFS = (0.75, -0.15, 1.0 / 60.0)
GAMMA_LESS = 0.4
HIGHEST = lax.Precision.HIGHEST


def padded_2(x, sides, width, wrap):
    for axis, dim in sides:
        devices, length = (lax.axis_size(axis), x.shape[dim])
        up = [(i, (i + 1) % devices) for i in range(devices if wrap else devices - 1)]
        down = [(j, i) for i, j in up]
        last = lax.slice_in_dim(x, length - width, length, axis=dim)
        leading = lax.slice_in_dim(x, 0, width, axis=dim)
        before = lax.ppermute(last, axis, up)
        after = lax.ppermute(leading, axis, down)
        x = jnp.concatenate([before, x, after], axis=dim)
    return x


def from_partner(x, axis, apart):
    return lax.ppermute(x, axis, [(i, i ^ 1 << apart) for i in range(lax.axis_size(axis))])


def spectral_table(count):
    points = np.arange(count)
    spread = points[:, None] - points[None, :]
    nonzero = np.where(spread == 0, 1, spread)
    entries = 0.5 * np.where(spread % 2 == 0, 1.0, -1.0) / np.sin(np.pi * nonzero / count)
    return jnp.asarray(np.where(spread == 0, 0.0, entries), jnp.float32)


def fluxes(density, moments):
    axial_m = moments[:, 0]
    radial_m = moments[:, 1]
    pitch_m = moments[:, 2]
    energy = moments[:, 3]
    pressure = GAMMA_LESS * (
        energy - 0.5 * (axial_m * axial_m + radial_m * radial_m + pitch_m * pitch_m) / density
    )
    pitch_v = pitch_m / density
    radial_v = radial_m / density
    along_pitch = jnp.stack(
        [
            pitch_m,
            axial_m * pitch_v,
            radial_m * pitch_v,
            pitch_m * pitch_v + pressure,
            (energy + pressure) * pitch_v,
        ],
        axis=1,
    )
    along_radial = jnp.stack(
        [
            radial_m,
            axial_m * radial_v,
            radial_m * radial_v + pressure,
            pitch_m * radial_v,
            (energy + pressure) * radial_v,
        ],
        axis=1,
    )
    return (along_pitch, along_radial)


def stencil(padded, axis, length):
    summed = None
    for offset, weight in enumerate(COEFFS):
        reach = offset + 1
        ahead = lax.slice_in_dim(padded, 3 + reach, 3 + reach + length, axis=axis)
        behind = lax.slice_in_dim(padded, 3 - reach, 3 - reach + length, axis=axis)
        term = weight * (ahead - behind)
        summed = term if summed is None else summed + term
    return summed


def pitch_derivative(along_pitch):
    width = along_pitch.shape[-1]
    edges = jnp.concatenate([along_pitch[..., :3], along_pitch[..., width - 3 :]], axis=4)
    rims = padded_2(edges, (("pitch", 4),), 3, True)
    inner = None
    for offset, weight in enumerate(COEFFS):
        reach = offset + 1
        term = weight * (
            jnp.roll(along_pitch, -reach, axis=4) - jnp.roll(along_pitch, reach, axis=4)
        )
        inner = term if inner is None else inner + term
    left_strip = jnp.concatenate([rims[..., 0:3], along_pitch[..., :6]], axis=4)
    right_strip = jnp.concatenate([along_pitch[..., width - 6 :], rims[..., 9:12]], axis=4)
    left_cols = stencil(left_strip, 4, 3)
    right_cols = stencil(right_strip, 4, 3)
    pad_none = ((0, 0),) * 4
    left_full = jnp.pad(left_cols, pad_none + ((0, width - 3),))
    right_full = jnp.pad(right_cols, pad_none + ((width - 3, 0),))
    column = jnp.arange(width)
    return jnp.where(column < 3, left_full, jnp.where(column >= width - 3, right_full, inner))


def cut_rows(joined, starts, width):
    pieces = []
    for member in range(joined.shape[0]):
        opening = starts[member]
        pieces.append(lax.dynamic_slice_in_dim(joined[member], opening, width, axis=2))
    return jnp.stack(pieces, axis=0)


def carry_in(sums, backward, width, decay):
    count_p = lax.axis_size("pitch")
    place = lax.axis_index("pitch")
    step_log = width * math.log(decay)
    wrap_gain = 1.0 / (1.0 - decay ** (width * count_p))
    every = lax.all_gather(sums[None], "pitch", axis=0, tiled=True)
    others = jnp.arange(count_p, dtype=jnp.int32)
    if backward:
        spacing = (others - place - 1) % count_p
    else:
        spacing = (place - others - 1) % count_p
    weights = jnp.exp(spacing.astype(jnp.float32) * step_log) * wrap_gain
    return jnp.dot(weights, every, precision=HIGHEST, preferred_element_type=jnp.float32)


def smooth(residual):
    width = residual.shape[-1]
    extent = width * lax.axis_size("pitch")
    smooth_eps = float(extent * extent // 16)
    decay = 2.0 * smooth_eps / (1.0 + 2.0 * smooth_eps + math.sqrt(1.0 + 4.0 * smooth_eps))
    points = np.arange(width)
    spacing = points[None, :] - points[:, None]
    lower = np.where(spacing >= 0, decay ** np.maximum(spacing, 0), 0.0)
    forward_table = jnp.asarray(lower, jnp.float32)
    backward_table = jnp.asarray(lower.T, jnp.float32)
    rising = jnp.asarray(decay ** (points + 1.0), jnp.float32)
    falling = jnp.asarray(decay ** (width - points + 0.0), jnp.float32)
    flat = residual.reshape(-1, width)
    first_pass = jnp.dot(flat, forward_table, precision=HIGHEST, preferred_element_type=jnp.float32)
    carried = carry_in(first_pass[:, -1], False, width, decay)
    swept = first_pass + carried[:, None] * rising[None, :]
    second_pass = jnp.dot(
        swept, backward_table, precision=HIGHEST, preferred_element_type=jnp.float32
    )
    carried_back = carry_in(second_pass[:, 0], True, width, decay)
    result = (second_pass + carried_back[:, None] * falling[None, :]) * (decay / smooth_eps)
    return result.reshape(residual.shape)


def local(density, moments, shifts):
    fields = jnp.concatenate([density[:, None], moments], axis=1)
    along_pitch, along_radial = fluxes(density, moments)
    count_p = lax.axis_size("pitch")
    place = lax.axis_index("pitch")
    width = density.shape[-1]
    planes = density.shape[1]
    padded_r = padded_2(along_radial, (("radial", 3),), 3, False)
    residual = pitch_derivative(along_pitch) + stencil(padded_r, 3, density.shape[2])
    residual = residual + jnp.einsum(
        "nm,mvarp->nvarp", spectral_table(fields.shape[0]), fields, precision=HIGHEST
    )
    stator = lax.axis_index("axial") == 1
    edge = jnp.where(stator, fields[:, :, 0], fields[:, :, planes - 1])
    facing = from_partner(edge, "axial", 0)
    extent = width * count_p
    offsets = jnp.where(stator, shifts, (extent - shifts) % extent)
    whole = lax.all_gather(facing, "pitch", axis=3, tiled=True)
    joined = jnp.concatenate([whole, whole], axis=3)
    aligned = cut_rows(joined, (place * width - offsets) % extent, width)
    penalty = aligned - edge
    target = jnp.where(stator, 0, planes - 1)
    chosen = (jnp.arange(planes) == target).astype(jnp.float32)
    residual = residual + penalty[:, :, None] * chosen[None, None, :, None, None]
    update = smooth(residual)
    return (residual, update)


def solution(mesh):
    in_specs = (P(None, "axial", "radial", "pitch"), P(None, None, "axial", "radial", "pitch"), P())
    out_specs = (
        P(None, None, "axial", "radial", "pitch"),
        P(None, None, "axial", "radial", "pitch"),
    )
    return jax.shard_map(local, mesh=mesh, in_specs=in_specs, out_specs=out_specs, check_vma=False)
```

profile of v0, /device:TPU:0, one launch (start us, length us, event | category | flops | bytes accessed | tf_op | source)
XLA Modules:
  0.0 217.8 jit_solution(8303843082527877109)
XLA Ops:
  0.6 1.1 copy.155
  1.8 1.0 copy.166
  2.9 3.0 %collective-permute-start.4 = (f32[9,5,8,128]{3,0,2,1:T(8,128)S(1)}, f32[9,5,8,128]{3,0,2,1:T(8,128)}, u32[]{:S(2)}, u32[]{:S(2)}) collective-permute-start(f32[9,5,8,128]{3,0,2,1:T(8,128)S(1)} %bitcast.141), channel_id=1, source_target_pairs={{0,1},{1,0},{2,3},{3,2},{4,5},{5,4},{6,7},{7,6},{8,9},{9,8},{10,11... | collective-permute-start | bytes 552968 | tf_op jit(solution)/shard_map/ppermute | solution.py:28
  5.9 1.7 fusion.103
  7.5 1.3 copy.143
  9.2 1.0 constant_dynamic-update-slice_fusion
  10.3 1.3 copy.162
  11.6 1.3 copy.163
  12.9 1.1 constant_dynamic-update-slice_fusion.1
  14.0 2.4 %fusion.24 = f32[9,2,8,128]{0,2,3,1:T(8,128)} fusion(f32[9,1,2,8,128]{0,3,4,2,1:T(8,128)S(1)} %copy.163, f32[9,1,2,8,128]{0,3,4,2,1:T(8,128)S(1)} %copy.161, f32[9,1,2,8,128]{0,3,4,2,1:T(8,128)} %copy.162), kind=kLoop, calls=%fused_computation.55 | loop fusion | flops 92160 | bytes 294912 | tf_op jit(solution)/shard_map/add | solution.py:45
  16.3 2.2 copy.146
  18.5 1.5 multiply_divide_fusion
  20.0 2.2 %copy.148 = f32[9,2,8,128]{0,2,3,1:T(8,128)} copy(f32[9,2,8,128]{3,2,1,0:T(8,128)} %multiply_divide_fusion) | data formatting | bytes 147456 | tf_op jit(solution)/shard_map/div | solution.py:45
  22.2 2.3 %copy.164 = f32[9,1,2,8,128]{0,3,4,2,1:T(8,128)} copy(f32[9,1,2,8,128]{4,3,2,1,0:T(8,128)} %get-tuple-element.47) | data formatting | bytes 147456
  24.6 2.5 %bitcast_dynamic-update-slice_fusion.7 = f32[9,5,2,8,128]{0,3,4,2,1:T(8,128)} fusion(f32[9,5,2,8,128]{0,3,4,2,1:T(8,128)} %constant_dynamic-update-slice_fusion, f32[9,1,2,8,128]{0,3,4,2,1:T(8,128)} %copy.162, f32[9,2,8,128]{0,2,3,1:T(8,128)S(1)} %copy.143, f32[9,1,2,8,128]{0,3,4,2,1:T(8,128)S(1)} %copy.161), kind=kLoop, calls=%fused_computation.57 | loop fusion | flops 36864 | bytes 2244608
  27.1 2.8 %bitcast_dynamic-update-slice_fusion.6 = (f32[9,5,2,8,128]{0,3,4,2,1:T(8,128)}, f32[9,5,2,8,128]{0,3,4,2,1:T(8,128)}) fusion(f32[9,5,2,8,128]{0,3,4,2,1:T(8,128)} %bitcast_dynamic-update-slice_fusion.7, f32[9,1,2,8,128]{0,3,4,2,1:T(8,128)S(1)} %copy.163, f32[9,2,8,128]{0,2,3,1:T(8,128)S(1)} %copy.143, f32[9,1,2,8,128]{0,3,4,2,1:T(8,128)S(1)} %copy.161, ...), kind=kLoop, calls=%fused_computation.49 | loop fusion | flops 73728 | bytes 3366912
  29.8 1.3 bitcast_dynamic-update-slice_fusion.5
  31.2 1.5 copy-done
  32.7 1.4 bitcast_dynamic-update-slice_fusion.4
  34.1 1.7 fusion.95
  35.7 1.6 collective-permute-start
  37.3 2.2 %collective-permute-start.1 = (f32[9,5,2,8,3]{0,3,4,2,1:T(8,128)}, f32[9,5,2,8,3]{0,3,4,2,1:T(8,128)}, u32[]{:S(2)}, u32[]{:S(2)}) collective-permute-start(f32[9,5,2,8,3]{0,3,4,2,1:T(8,128)} %get-tuple-element.21), channel_id=1, source_target_pairs={{8,0},{16,8},{24,16},{0,24},{9,1},{17,9},{25,17},{1,25},{10,2},{18... | collective-permute-start | bytes 25928 | tf_op jit(solution)/shard_map/ppermute | solution.py:22
  40.0 2.3 %copy-done.1 = f32[9,5,2,8,128]{0,3,4,2,1:T(8,128)} copy-done((f32[9,5,2,8,128]{0,3,4,2,1:T(8,128)}, f32[9,5,2,8,128]{0,3,4,2,1:T(8,128)S(1)}, u32[]{:S(2)}) %copy-start.1) | copy-done | bytes 368664
  42.4 2.6 %fusion.101 = (f32[9,5,2,3,128]{0,3,4,2,1:T(4,128)}, f32[9,5,2,3,128]{0,3,4,2,1:T(4,128)S(1)}) fusion(f32[9,5,2,8,128]{0,3,4,2,1:T(8,128)S(1)} %bitcast_dynamic-update-slice_fusion), kind=kLoop, calls=%fused_computation.182 | loop fusion | bytes 552960 | tf_op jit(solution)/shard_map/slice | solution.py:20
  44.9 2.9 %copy.150 = f32[9,5,2,3,128]{4,2,3,1,0:T(2,128)S(1)} copy(f32[9,5,2,3,128]{0,3,4,2,1:T(4,128)} %get-tuple-element.32) | data formatting | bytes 276480 | tf_op jit(solution)/shard_map/slice | solution.py:20
  47.8 1.3 collective-permute-start.2
  49.1 2.2 %copy.152 = f32[9,5,2,3,128]{4,2,3,1,0:T(2,128)} copy(f32[9,5,2,3,128]{0,3,4,2,1:T(4,128)S(1)} %get-tuple-element.33) | data formatting | bytes 276480 | tf_op jit(solution)/shard_map/slice | solution.py:19
  51.3 3.7 %collective-permute-start.3 = (f32[9,5,2,3,128]{4,2,3,1,0:T(2,128)}, f32[9,5,2,3,128]{4,2,3,1,0:T(2,128)}, u32[]{:S(2)}, u32[]{:S(2)}) collective-permute-start(f32[9,5,2,3,128]{4,2,3,1,0:T(2,128)} %copy.152), channel_id=1, source_target_pairs={{0,2},{2,4},{4,6},{1,3},{3,5},{5,7},{8,10},{10,12},{12,14},{9,11},... | collective-permute-start | bytes 414728 | tf_op jit(solution)/shard_map/ppermute | solution.py:21
  55.0 1.2 fusion.94
  56.3 8.9 %fusion.100 = (f32[9,5,2,8,127]{0,3,4,2,1:T(8,128)}, f32[9,5,2,8,127]{0,3,4,2,1:T(8,128)}) fusion(f32[9,5,2,8,128]{0,3,4,2,1:T(8,128)} %get-tuple-element.34), kind=kLoop, calls=%fused_computation.181 | loop fusion | bytes 1463040 | tf_op jit(solution)/shard_map/jit(_roll_static)/slice | solution.py:91
  65.2 4.6 %fusion.98 = (f32[9,5,2,8,126]{0,3,4,2,1:T(8,128)}, f32[9,5,2,8,126]{0,3,4,2,1:T(8,128)}) fusion(f32[9,5,2,8,128]{0,3,4,2,1:T(8,128)S(1)} %bitcast.139), kind=kLoop, calls=%fused_computation.179 | loop fusion | bytes 1451520 | tf_op jit(solution)/shard_map/jit(_roll_static)/slice | solution.py:91
  69.8 4.5 %fusion.96 = (f32[9,5,2,8,125]{0,3,4,2,1:T(8,128)}, f32[9,5,2,8,125]{0,3,4,2,1:T(8,128)}) fusion(f32[9,5,2,8,128]{0,3,4,2,1:T(8,128)S(1)} %bitcast.139), kind=kLoop, calls=%fused_computation.177 | loop fusion | bytes 1440000 | tf_op jit(solution)/shard_map/jit(_roll_static)/slice | solution.py:91
  87.9 3.2 %copy.156 = f32[9,5,2,8,128]{0,3,4,2,1:T(8,128)} copy(f32[9,5,2,8,128]{4,0,3,2,1:T(8,128)S(1)} %fusion.27) | data formatting | bytes 737280 | tf_op jit(solution)/shard_map/nm,mvarp->nvarp/dot_general | solution.py:161
  97.8 2.1 fusion.42
  99.9 1.8 copy.151
  101.7 3.4 %copy.153 = f32[9,5,2,3,128]{0,3,4,2,1:T(4,128)} copy(f32[9,5,2,3,128]{4,2,3,1,0:T(2,128)} %collective-permute-done.3) | data formatting | bytes 276480 | tf_op jit(solution)/shard_map/ppermute | solution.py:21
  105.1 26.5 %all_gather.9 = f32[9,5,8,512]{3,0,2,1:T(8,128)S(1)} all-gather(f32[9,5,8,128]{3,0,2,1:T(8,128)} %collective-permute-done.4), channel_id=1, replica_groups=mesh['pitch'=4,'radial'=4,'axial'=2] {'pitch'}, dimensions={3}, use_global_device_ids=true | all-gather | bytes 921600 | tf_op jit(solution)/shard_map/all_gather | solution.py:169
  131.9 1.2 fusion.102
  133.2 0.8 dynamic-slice_bitcast_fusion
  134.0 0.8 dynamic-slice_bitcast_fusion.2
  135.5 0.8 dynamic-slice_bitcast_fusion.6
  136.3 1.8 stack.79
  138.9 3.2 %copy.157 = f32[9,5,8,128]{0,2,3,1:T(8,128)} copy(f32[9,5,8,128]{3,0,2,1:T(8,128)} %subtract_bitcast_fusion) | data formatting | bytes 368640 | tf_op jit(solution)/shard_map/mul | solution.py:175
  142.1 35.6 %fusion.7 = f32[9,5,2,8,128]{0,3,4,2,1:T(8,128)} fusion(f32[9,5,2,8,128]{0,3,4,2,1:T(8,128)} %copy.156, f32[9,5,2,8,128]{0,3,4,2,1:T(8,128)} %copy-done.1, f32[9,5,2,3,128]{0,3,4,2,1:T(4,128)} %copy.153, f32[9,5,2,3,128]{0,3,4,2,1:T(4,128)S(1)} %copy.151, f32[9,5,2,8,1]{0,3,4,2,1:T(8,128)} %get-tuple-element.29, f32[9,5,2,8,127]{0,3,4,2,1:T(8,128)} %get-tuple-element.31, ...), kind=kLoop, calls=%fused_computation.15 | loop fusion | flops 3133440 | bytes 3796104 | tf_op jit(solution)/shard_map/add | solution.py:175
  177.7 3.4 %copy.159 = f32[9,5,2,8,128]{4,3,2,1,0:T(8,128)S(1)} copy(f32[9,5,2,8,128]{0,3,4,2,1:T(8,128)} %fusion.7) | data formatting | bytes 737280
  182.2 17.6 %all-reduce.2 = f32[2880]{0:T(1024)S(1)} all-reduce(f32[2880]{0:T(1024)S(1)} %dynamic-update-slice), channel_id=2, replica_groups=mesh['pitch'=4,'radial'=4,'axial'=2] {'pitch'}, use_global_device_ids=true, to_apply=%add.2 | all-reduce | flops 2880 | bytes 23040
  201.0 15.5 %all-reduce.3 = f32[2880]{0:T(1024)S(1)} all-reduce(f32[2880]{0:T(1024)S(1)} %dynamic-update-slice.1), channel_id=3, replica_groups=mesh['pitch'=4,'radial'=4,'axial'=2] {'pitch'}, use_global_device_ids=true, to_apply=%add.3 | all-reduce | flops 2880 | bytes 23040
  216.8 0.9 add_multiply_fusion
  (71 shorter events, 8.7 us)
Async XLA Ops:
  1.8 4.1 %copy-start.4 = (f32[9,4,2,8,128]{4,0,3,2,1:T(8,128)}, f32[9,4,2,8,128]{4,0,3,2,1:T(8,128)S(1)}, u32[]{:S(2)}) copy-start(f32[9,4,2,8,128]{4,0,3,2,1:T(8,128)S(1)} %copy.155) | copy-start | bytes 884740
  2.8 3.1 %copy-start.7 = (f32[9,2,8,128]{3,0,2,1:T(8,128)}, f32[9,2,8,128]{3,0,2,1:T(8,128)S(1)}, u32[]{:S(2)}) copy-start(f32[9,2,8,128]{3,0,2,1:T(8,128)S(1)} %copy.166) | copy-start | bytes 221188
  2.9 102.3 %collective-permute-start.4 = (f32[9,5,8,128]{3,0,2,1:T(8,128)S(1)}, f32[9,5,8,128]{3,0,2,1:T(8,128)}, u32[]{:S(2)}, u32[]{:S(2)}) collective-permute-start(f32[9,5,8,128]{3,0,2,1:T(8,128)S(1)} %bitcast.141), channel_id=1, source_target_pairs={{0,1},{1,0},{2,3},{3,2},{4,5},{5,4},{6,7},{7,6},{8,9},{9,8},{10,11... | collective-permute-start | bytes 552968 | tf_op jit(solution)/shard_map/ppermute | solution.py:28
  10.3 8.2 %copy-start.9 = (f32[9,2,8,128]{3,2,1,0:T(8,128)S(1)}, f32[9,2,8,128]{3,2,1,0:T(8,128)}, u32[]{:S(2)}) copy-start(f32[9,2,8,128]{3,2,1,0:T(8,128)} %param.8) | copy-start | bytes 221188
  24.6 5.3 %copy-start.2 = (f32[9,2,8,128]{0,2,3,1:T(8,128)S(1)}, f32[9,2,8,128]{0,2,3,1:T(8,128)}, u32[]{:S(2)}) copy-start(f32[9,2,8,128]{0,2,3,1:T(8,128)} %copy.148) | copy-start | bytes 221188
  24.6 5.3 %copy-start.3 = (f32[9,1,2,8,128]{0,3,4,2,1:T(8,128)S(1)}, f32[9,1,2,8,128]{0,3,4,2,1:T(8,128)}, u32[]{:S(2)}) copy-start(f32[9,1,2,8,128]{0,3,4,2,1:T(8,128)} %copy.164) | copy-start | bytes 221188
  29.8 2.9 %copy-start = (f32[9,5,2,8,128]{0,3,4,2,1:T(8,128)S(1)}, f32[9,5,2,8,128]{0,3,4,2,1:T(8,128)}, u32[]{:S(2)}) copy-start(f32[9,5,2,8,128]{0,3,4,2,1:T(8,128)} %get-tuple-element.46) | copy-start | bytes 1105924
  35.7 62.1 %collective-permute-start = (f32[9,5,2,8,3]{0,3,4,2,1:T(8,128)}, f32[9,5,2,8,3]{0,3,4,2,1:T(8,128)}, u32[]{:S(2)}, u32[]{:S(2)}) collective-permute-start(f32[9,5,2,8,3]{0,3,4,2,1:T(8,128)} %get-tuple-element.20), channel_id=1, source_target_pairs={{0,8},{8,16},{16,24},{24,0},{1,9},{9,17},{17,25},{25,1},{2,10},{10... | collective-permute-start | bytes 25928 | tf_op jit(solution)/shard_map/ppermute | solution.py:21
  37.3 60.5 %collective-permute-start.1 = (f32[9,5,2,8,3]{0,3,4,2,1:T(8,128)}, f32[9,5,2,8,3]{0,3,4,2,1:T(8,128)}, u32[]{:S(2)}, u32[]{:S(2)}) collective-permute-start(f32[9,5,2,8,3]{0,3,4,2,1:T(8,128)} %get-tuple-element.21), channel_id=1, source_target_pairs={{8,0},{16,8},{24,16},{0,24},{9,1},{17,9},{25,17},{1,25},{10,2},{18... | collective-permute-start | bytes 25928 | tf_op jit(solution)/shard_map/ppermute | solution.py:22
  40.0 2.3 %copy-start.1 = (f32[9,5,2,8,128]{0,3,4,2,1:T(8,128)}, f32[9,5,2,8,128]{0,3,4,2,1:T(8,128)S(1)}, u32[]{:S(2)}) copy-start(f32[9,5,2,8,128]{0,3,4,2,1:T(8,128)S(1)} %bitcast_dynamic-update-slice_fusion) | copy-start | bytes 1105924
  47.8 52.1 %collective-permute-start.2 = (f32[9,5,2,3,128]{4,2,3,1,0:T(2,128)S(1)}, f32[9,5,2,3,128]{4,2,3,1,0:T(2,128)S(1)}, u32[]{:S(2)}, u32[]{:S(2)}) collective-permute-start(f32[9,5,2,3,128]{4,2,3,1,0:T(2,128)S(1)} %copy.150), channel_id=1, source_target_pairs={{2,0},{4,2},{6,4},{3,1},{5,3},{7,5},{10,8},{12,10},{14,12},{11,9},... | collective-permute-start | bytes 414728 | tf_op jit(solution)/shard_map/ppermute | solution.py:22
  51.3 50.4 %collective-permute-start.3 = (f32[9,5,2,3,128]{4,2,3,1,0:T(2,128)}, f32[9,5,2,3,128]{4,2,3,1,0:T(2,128)}, u32[]{:S(2)}, u32[]{:S(2)}) collective-permute-start(f32[9,5,2,3,128]{4,2,3,1,0:T(2,128)} %copy.152), channel_id=1, source_target_pairs={{0,2},{2,4},{4,6},{1,3},{3,5},{5,7},{8,10},{10,12},{12,14},{9,11},... | collective-permute-start | bytes 414728 | tf_op jit(solution)/shard_map/ppermute | solution.py:21
  55.0 10.2 %slice-start = ((s8[5242880]{0:T(1024)(128)(4,1)}), s8[4194304]{0:T(1024)(128)(4,1)S(1)}, s32[]{:S(2)}) async-start(s8[5242880]{0:T(1024)(128)(4,1)} %bitcast.138), calls=%async_computation | async-start | bytes 8388608
  56.3 8.9 %slice-start.1 = ((s8[5242880]{0:T(1024)(128)(4,1)}), s8[1048576]{0:T(1024)(128)(4,1)S(1)}, s32[]{:S(2)}) async-start(s8[5242880]{0:T(1024)(128)(4,1)} %bitcast.138), calls=%async_computation.1 | async-start | bytes 2097152
  69.8 5.8 %copy-start.14 = (s32[9]{0:T(128)S(1)}, s32[9]{0:T(128)}, u32[]{:S(2)}) copy-start(s32[9]{0:T(128)} %param.10) | copy-start | bytes 112
  69.8 6.5 %copy-start.5 = (f32[9,4,2,8,128]{4,0,3,2,1:T(8,128)S(1)}, f32[9,4,2,8,128]{4,0,3,2,1:T(8,128)}, u32[]{:S(2)}) copy-start(f32[9,4,2,8,128]{4,0,3,2,1:T(8,128)} %copy-done.4) | copy-start | bytes 884740
  69.8 6.5 %copy-start.8 = (f32[9,2,8,128]{3,0,2,1:T(8,128)S(1)}, f32[9,2,8,128]{3,0,2,1:T(8,128)}, u32[]{:S(2)}) copy-start(f32[9,2,8,128]{3,0,2,1:T(8,128)} %copy-done.7) | copy-start | bytes 221188
  69.8 6.5 %copy-start.12 = (f32[9,9,1,1,1]{1,0,4,3,2:T(8,128)S(1)}, f32[9,9,1,1,1]{1,0,4,3,2:T(8,128)}, u32[]{:S(2)}) copy-start(f32[9,9,1,1,1]{1,0,4,3,2:T(8,128)} %constant.124) | copy-start | bytes 976
  74.3 22.3 %copy-start.16 = (u32[32]{0:T(128)S(1)}, u32[32]{0:T(128)}, u32[]{:S(2)}) copy-start(u32[32]{0:T(128)} %constant.114) | copy-start | bytes 388
  177.7 3.4 %copy-start.10 = (f32[128,128]{1,0:T(8,128)S(1)}, f32[128,128]{1,0:T(8,128)}, u32[]{:S(2)}) copy-start(f32[128,128]{1,0:T(8,128)} %constant.104.clone) | copy-start | bytes 196612
  177.7 22.3 %copy-start.11 = (f32[128,128]{1,0:T(8,128)S(1)}, f32[128,128]{1,0:T(8,128)}, u32[]{:S(2)}) copy-start(f32[128,128]{1,0:T(8,128)} %constant.105.clone) | copy-start | bytes 196612
  177.7 22.3 %copy-start.15 = (f32[128]{0:T(128)S(1)}, f32[128]{0:T(128)}, u32[]{:S(2)}) copy-start(f32[128]{0:T(128)} %constant.106.clone) | copy-start | bytes 1540
  177.7 39.1 %copy-start.13 = (f32[128]{0:T(128)S(1)}, f32[128]{0:T(128)}, u32[]{:S(2)}) copy-start(f32[128]{0:T(128)} %constant.107.clone) | copy-start | bytes 1540
  181.1 36.7 %copy-start.6 = (f32[9,5,2,8,128]{4,3,2,1,0:T(8,128)}, f32[9,5,2,8,128]{4,3,2,1,0:T(8,128)S(1)}, u32[]{:S(2)}) copy-start(f32[9,5,2,8,128]{4,3,2,1,0:T(8,128)S(1)} %copy.159) | copy-start | bytes 1105924
where the time goes:
time: 219 us; the launch traced here: 218 us
  local copies, waits for them, and re-layouts  74.5 us (34%)
  blocking collectives  59.6 us (27%)
  other arithmetic  51.7 us (24%)
  between operations  18.1 us (8%)
  starting transfers between devices  11.8 us (5%)
    add x1, other arithmetic, local(): residual + penalty[:, :, None] * chosen[None, None, :, None, None]  35.6 us
    unnamed x2, blocking collectives  33.1 us
    all_gather x1, blocking collectives, local(): whole = lax.all_gather(facing, 'pitch', axis=3, tiled=True)  26.5 us
    unnamed x54, local copies, waits for them, and re-layouts  19.5 us
    slice x5, local copies, waits for them, and re-layouts, pitch_derivative(): jnp.roll(along_pitch, reach, axis=4)  19.2 us
    unnamed x5, other arithmetic  6.74 us
    slice x2, local copies, waits for them, and re-layouts, padded_2(): leading = lax.slice_in_dim(x, 0, width, axis=dim)  5.42 us
    ppermute x2, starting transfers between devices, padded_2(): before = lax.ppermute(last, axis, up)  5.27 us
  transfers between devices with their start and end apart: 5, of which 0 were waited for; matrix products, arithmetic and copies ran while one was open for 32% of the time, Pallas kernels for 0%

commit v1 on v0

v1 whole, which is shorter than its diff:
```python
import functools
import math

import jax
import jax.numpy as jnp
import numpy as np
from jax import lax
from jax.experimental import pallas as pl
from jax.experimental.pallas import tpu as pltpu
from jax.sharding import PartitionSpec as P

COEFFS = (0.75, -0.15, 1.0 / 60.0)
GAMMA_LESS = 0.4
HIGHEST = lax.Precision.HIGHEST
MESH = pl.DeviceIdType.MESH
VMEM = pl.BlockSpec(memory_space=pltpu.VMEM)
SMEM = pl.BlockSpec(memory_space=pltpu.SMEM)
CHUNKS = 3


def filter_constants(extent):
    eps = float(extent * extent // 16)
    decay = 2.0 * eps / (1.0 + 2.0 * eps + math.sqrt(1.0 + 4.0 * eps))
    gain = 1.0 / (math.sqrt(1.0 + 4.0 * eps) * (1.0 - decay**extent))
    return decay, gain


def tables(width, extent):
    decay, gain = filter_constants(extent)
    points = np.arange(width)
    apart = np.abs(points[:, None] - points[None, :])
    green = gain * (decay**apart + decay ** (extent - apart))
    deriv = np.zeros((width, width))
    rims = np.zeros((8, width))
    picks = np.zeros((8, width))
    for offset, weight in enumerate(COEFFS):
        reach = offset + 1
        for i in range(width):
            if i + reach < width:
                deriv[i + reach, i] += weight
            else:
                rims[i + reach - width, i] += weight
            if i - reach >= 0:
                deriv[i - reach, i] -= weight
            else:
                rims[4 + i - reach + 3, i] -= weight
    for h in range(3):
        picks[h, h] = 1.0
        picks[4 + h, width - 3 + h] = 1.0
    sums = np.zeros((8, width))
    sums[0] = decay ** (width - 1.0 - points)
    sums[1] = decay ** (points + 0.0)
    spread = np.zeros((8, width))
    spread[0] = gain * decay ** (points + 1.0)
    spread[1] = gain * decay ** (width - points + 0.0)
    return np.concatenate([deriv, green, rims, picks, sums, spread]).astype(np.float32)


def dot(a, b):
    return jnp.dot(a, b, precision=HIGHEST, preferred_element_type=jnp.float32)


def dot_nt(a, b):
    return lax.dot_general(
        a, b, (((1,), (1,)), ((), ())), precision=HIGHEST, preferred_element_type=jnp.float32
    )


def dot_tn(a, b):
    return lax.dot_general(
        a, b, (((0,), (0,)), ((), ())), precision=HIGHEST, preferred_element_type=jnp.float32
    )


def exchange_kernel(
    count_p,
    count_r,
    density,
    moments,
    table,
    base,
    smoothed,
    whole,
    along_p,
    along_r,
    rim_out,
    rim_in,
    sum_out,
    sum_in,
    cross_send,
    cross_recv,
    chain_send,
    chain_recv,
    rim_send,
    rim_recv,
    radial_send,
    radial_recv,
    sum_send,
    sum_recv,
):
    inst, planes, rad, width = density.shape
    rows = inst * 5 * planes * rad
    extent = width * count_p
    decay, _ = filter_constants(extent)
    p = lax.axis_index("pitch")
    r = lax.axis_index("radial")
    a = lax.axis_index("axial")
    plane = (planes - 1) * (1 - a)
    per = inst // CHUNKS

    barrier = pltpu.get_barrier_semaphore()
    for k in range(1, count_p):
        pl.semaphore_signal(
            barrier, inc=1, device_id=(lax.rem(p + k, count_p), r, a), device_id_type=MESH
        )
    for k in (1, count_r - 1):
        pl.semaphore_signal(
            barrier, inc=1, device_id=(p, lax.rem(r + k, count_r), a), device_id_type=MESH
        )
    pl.semaphore_signal(barrier, inc=1, device_id=(p, r, 1 - a), device_id_type=MESH)

    rho = density[...]
    axial_m, radial_m, pitch_m, energy = (moments[:, v] for v in range(4))
    inverse = 1.0 / rho
    pressure = GAMMA_LESS * (
        energy - 0.5 * (axial_m * axial_m + radial_m * radial_m + pitch_m * pitch_m) * inverse
    )
    pitch_v = pitch_m * inverse
    radial_v = radial_m * inverse
    enthalpy = energy + pressure
    along_p[:, 0] = pitch_m
    along_p[:, 1] = axial_m * pitch_v
    along_p[:, 2] = radial_m * pitch_v
    along_p[:, 3] = pitch_m * pitch_v + pressure
    along_p[:, 4] = enthalpy * pitch_v
    mine = slice(rad, 2 * rad)
    along_r[:, 0, :, mine] = radial_m
    along_r[:, 1, :, mine] = axial_m * radial_v
    along_r[:, 2, :, mine] = radial_m * radial_v + pressure
    along_r[:, 3, :, mine] = pitch_m * radial_v
    along_r[:, 4, :, mine] = enthalpy * radial_v

    @pl.when(r == 0)
    def _():
        along_r[:, :, :, 0:rad] = jnp.zeros((inst, 5, planes, rad, width), jnp.float32)

    @pl.when(r == count_r - 1)
    def _():
        along_r[:, :, :, 2 * rad : 3 * rad] = jnp.zeros(
            (inst, 5, planes, rad, width), jnp.float32
        )

    pl.semaphore_wait(barrier, count_p + 2)

    def cross(c, part):
        span = pl.ds(c * per, per)
        if part == 0:
            src, dst = density.at[span, plane], whole.at[p, span, 0]
        else:
            src, dst = moments.at[span, :, plane], whole.at[p, span, 1:5]
        return pltpu.make_async_remote_copy(
            src_ref=src,
            dst_ref=dst,
            send_sem=cross_send.at[c, part],
            recv_sem=cross_recv.at[c, part],
            device_id=(p, r, 1 - a),
            device_id_type=MESH,
        )

    for c in range(CHUNKS):
        for part in range(2):
            cross(c, part).start()

    def radial_copy(up):
        if up:
            src = along_r.at[:, :, :, 2 * rad - 3 : 2 * rad]
            dst = along_r.at[:, :, :, rad - 3 : rad]
            target = r + 1
        else:
            src = along_r.at[:, :, :, rad : rad + 3]
            dst = along_r.at[:, :, :, 2 * rad : 2 * rad + 3]
            target = r - 1
        return pltpu.make_async_remote_copy(
            src_ref=src,
            dst_ref=dst,
            send_sem=radial_send.at[int(up)],
            recv_sem=radial_recv.at[int(up)],
            device_id=(p, target, a),
            device_id_type=MESH,
        )

    @pl.when(r < count_r - 1)
    def _():
        radial_copy(True).start()

    @pl.when(r > 0)
    def _():
        radial_copy(False).start()

    flat_p = along_p[...].reshape(rows, width)
    rim_out[...] = dot_nt(table[2 * width + 8 : 2 * width + 16], flat_p)

    def rim_copy(up):
        part = slice(4, 8) if up else slice(0, 4)
        return pltpu.make_async_remote_copy(
            src_ref=rim_out.at[part],
            dst_ref=rim_in.at[part],
            send_sem=rim_send.at[int(up)],
            recv_sem=rim_recv.at[int(up)],
            device_id=(lax.rem(p + (1 if up else count_p - 1), count_p), r, a),
            device_id_type=MESH,
        )

    rim_copy(True).start()
    rim_copy(False).start()

    def chain(s, c, up):
        block = p - (s - 1) if up else p + (s - 1)
        span = pl.ds(c * per, per)
        part = whole.at[block, span]
        return pltpu.make_async_remote_copy(
            src_ref=part,
            dst_ref=part,
            send_sem=chain_send.at[int(up), s - 1, c],
            recv_sem=chain_recv.at[int(up), s - 1, c],
            device_id=(p + 1 if up else p - 1, r, a),
            device_id_type=MESH,
        )

    def arrival(s, c, up):
        block = p - s if up else p + s
        span = pl.ds(c * per, per)
        part = whole.at[block, span]
        return pltpu.make_async_remote_copy(
            src_ref=part,
            dst_ref=part,
            send_sem=chain_send.at[int(up), s - 1, c],
            recv_sem=chain_recv.at[int(up), s - 1, c],
            device_id=(p - 1 if up else p + 1, r, a),
            device_id_type=MESH,
        )

    def sends(s, up):
        if up:
            return jnp.logical_and(p < count_p - 1, p - (s - 1) >= 0)
        return jnp.logical_and(p > 0, p + (s - 1) < count_p)

    def receives(s, up):
        return p - s >= 0 if up else p + s < count_p

    def first_step(c):
        cross(c, 0).wait_recv()
        cross(c, 1).wait_recv()
        for up in (True, False):
            pl.when(sends(1, up))(lambda up=up: chain(1, c, up).start())

    def later_step(s, c):
        for up in (True, False):
            pl.when(receives(s - 1, up))(lambda up=up: arrival(s - 1, c, up).wait_recv())
            pl.when(sends(s, up))(lambda up=up: chain(s, c, up).start())

    fields = [rho] + [axial_m, radial_m, pitch_m, energy]
    partial = dot(flat_p, table[0:width])
    base[...] = partial.reshape(inst, 5, planes, rad, width)
    for v, field in enumerate(fields):
        total = None
        for k in range(1, (inst + 1) // 2):
            weight = 0.5 * (-1.0) ** k / math.sin(math.pi * k / inst)
            back = jnp.concatenate([field[inst - k :], field[: inst - k]], axis=0)
            ahead = jnp.concatenate([field[k:], field[:k]], axis=0)
            term = weight * (back - ahead)
            total = term if total is None else total + term
        for b in range(planes):
            on = jnp.where(plane == b, 1.0, 0.0).astype(jnp.float32)
            base[:, v, b] += total[:, b] - on * field[:, b]

    first_step(0)

    pl.when(r > 0)(lambda: radial_copy(True).wait_recv())
    pl.when(r < count_r - 1)(lambda: radial_copy(False).wait_recv())
    rim_copy(True).wait_recv()
    rim_copy(False).wait_recv()
    across = dot_tn(rim_in[...], table[2 * width : 2 * width + 8])
    radial = None
    for offset, weight in enumerate(COEFFS):
        k = offset + 1
        term = weight * (
            along_r[:, :, :, rad + k : 2 * rad + k] - along_r[:, :, :, rad - k : 2 * rad - k]
        )
        radial = term if radial is None else radial + term
    base[...] += across.reshape(inst, 5, planes, rad, width) + radial
    flat = base[...].reshape(rows, width)
    sum_out[...] = dot_nt(table[2 * width + 16 : 2 * width + 24], flat)

    def sum_copy(k):
        return pltpu.make_async_remote_copy(
            src_ref=sum_out.at[0:2],
            dst_ref=sum_in.at[k - 1],
            send_sem=sum_send.at[k - 1],
            recv_sem=sum_recv.at[k - 1],
            device_id=(lax.rem(p + k, count_p), r, a),
            device_id_type=MESH,
        )

    for k in range(1, count_p):
        sum_copy(k).start()
    for c in range(1, CHUNKS):
        first_step(c)
    smoothed[...] = dot(flat, table[width : 2 * width]).reshape(inst, 5, planes, rad, width)
    for c in range(CHUNKS):
        later_step(2, c)
    ahead = None
    behind = None
    for k in range(1, count_p):
        sum_copy(k).wait_recv()
        left = decay ** (width * (k - 1.0)) * sum_in[k - 1, 0:1]
        right = decay ** (width * (count_p - k - 1.0)) * sum_in[k - 1, 1:2]
        ahead = left if ahead is None else ahead + left
        behind = right if behind is None else behind + right
    carried = jnp.concatenate([ahead, behind, jnp.zeros((6, rows), jnp.float32)], axis=0)
    smoothed[...] += dot_tn(carried, table[2 * width + 24 : 2 * width + 32]).reshape(
        inst, 5, planes, rad, width
    )
    for s in range(3, count_p):
        for c in range(CHUNKS):
            later_step(s, c)

    for c in range(CHUNKS):
        for up in (True, False):
            last = count_p - 1
            pl.when(receives(last, up))(
                lambda c=c, up=up: arrival(last, c, up).wait_recv()
            )
            for s in range(1, count_p):
                pl.when(sends(s, up))(lambda s=s, c=c, up=up: chain(s, c, up).wait_send())
        cross(c, 0).wait_send()
        cross(c, 1).wait_send()
    pl.when(r < count_r - 1)(lambda: radial_copy(True).wait_send())
    pl.when(r > 0)(lambda: radial_copy(False).wait_send())
    rim_copy(True).wait_send()
    rim_copy(False).wait_send()
    for k in range(1, count_p):
        sum_copy(k).wait_send()


def finish_kernel(
    count_p, shifts, table, whole, base, smoothed, residual, update, aligned, before, after
):
    inst, _, planes, rad, width = base.shape
    extent = width * count_p
    decay, _ = filter_constants(extent)
    log_decay = math.log(decay)
    p = lax.axis_index("pitch")
    a = lax.axis_index("axial")
    plane = (planes - 1) * (1 - a)
    lane = lax.broadcasted_iota(jnp.int32, (rad, width), 1)
    group = 5 * rad
    for n in range(inst):
        offset = jnp.where(a == 1, shifts[n], extent - shifts[n])
        start = lax.rem(p * width - offset + 2 * extent, extent)
        block = lax.div(start, width)
        inside = start - block * width
        near = whole[block, n]
        far = whole[lax.rem(block + 1, count_p), n]
        merged = jnp.where((lane >= inside)[None], near, far).reshape(group, width)
        aligned[n * group : (n + 1) * group] = pltpu.roll(
            merged, lax.rem(width - inside, width), 1
        )
        left = None
        right = None
        for b in range(count_p):
            spacing = start - 1 - b * width - lane
            spacing = jnp.where(spacing < 0, spacing + extent, spacing)
            outside = spacing < extent - width
            gap = spacing.astype(jnp.float32)
            up = jnp.where(outside, jnp.exp(gap * log_decay), 0.0)
            down = jnp.where(outside, jnp.exp((extent - width - 1.0 - gap) * log_decay), 0.0)
            block_b = whole[b, n]
            left = block_b * up[None] if left is None else left + block_b * up[None]
            right = block_b * down[None] if right is None else right + block_b * down[None]
        before[n * group : (n + 1) * group] = left.reshape(group, width)
        after[n * group : (n + 1) * group] = right.reshape(group, width)
    spread = table[2 * width + 24 : 2 * width + 32]
    ahead = jnp.sum(before[...], axis=1, keepdims=True)
    behind = jnp.sum(after[...], axis=1, keepdims=True)
    filtered = dot(aligned[...], table[width : 2 * width])
    filtered = filtered + ahead * spread[0:1] + behind * spread[1:2]
    shape = (inst, 5, rad, width)
    residual[...] = base[...]
    update[...] = smoothed[...]
    residual[:, :, plane] += aligned[...].reshape(shape)
    update[:, :, plane] += filtered.reshape(shape)


def local(density, moments, shifts):
    count_p = lax.axis_size("pitch")
    count_r = lax.axis_size("radial")
    inst, planes, rad, width = density.shape
    rows = inst * 5 * planes * rad
    table = jnp.asarray(tables(width, width * count_p))
    block = jax.ShapeDtypeStruct((inst, 5, planes, rad, width), jnp.float32)
    dma = pltpu.SemaphoreType.DMA
    base, smoothed, whole = pl.pallas_call(
        functools.partial(exchange_kernel, count_p, count_r),
        out_shape=(
            block,
            block,
            jax.ShapeDtypeStruct((count_p, inst, 5, rad, width), jnp.float32),
        ),
        in_specs=[VMEM] * 3,
        out_specs=(VMEM,) * 3,
        scratch_shapes=[
            pltpu.VMEM((inst, 5, planes, rad, width), jnp.float32),
            pltpu.VMEM((inst, 5, planes, 3 * rad, width), jnp.float32),
            pltpu.VMEM((8, rows), jnp.float32),
            pltpu.VMEM((8, rows), jnp.float32),
            pltpu.VMEM((8, rows), jnp.float32),
            pltpu.VMEM((count_p - 1, 2, rows), jnp.float32),
            dma((CHUNKS, 2)),
            dma((CHUNKS, 2)),
            dma((2, count_p - 1, CHUNKS)),
            dma((2, count_p - 1, CHUNKS)),
            dma((2,)),
            dma((2,)),
            dma((2,)),
            dma((2,)),
            dma((count_p - 1,)),
            dma((count_p - 1,)),
        ],
        compiler_params=pltpu.CompilerParams(
            collective_id=0, has_side_effects=True, vmem_limit_bytes=40 * 2**20
        ),
        name="exchange",
    )(density, moments, table)
    return pl.pallas_call(
        functools.partial(finish_kernel, count_p),
        out_shape=(block, block),
        in_specs=[SMEM] + [VMEM] * 4,
        out_specs=(VMEM,) * 2,
        scratch_shapes=[pltpu.VMEM((inst * 5 * rad, width), jnp.float32)] * 3,
        compiler_params=pltpu.CompilerParams(vmem_limit_bytes=40 * 2**20),
        name="finish",
    )(shifts, table, whole, base, smoothed)


def solution(mesh):
    in_specs = (P(None, "axial", "radial", "pitch"), P(None, None, "axial", "radial", "pitch"), P())
    out_specs = (
        P(None, None, "axial", "radial", "pitch"),
        P(None, None, "axial", "radial", "pitch"),
    )
    return jax.shard_map(local, mesh=mesh, in_specs=in_specs, out_specs=out_specs, check_vma=False)
```

time: 219 us -> 30.4 us (0.14)
  local copies, waits for them, and re-layouts: 74.5 us -> 3.39 us
  blocking collectives: 59.6 us -> 0 us
  other arithmetic: 51.7 us -> 0 us
  Pallas kernels: 0 us -> 26.2 us
  between operations: 18.1 us -> 0.66 us
  starting transfers between devices: 11.8 us -> 0 us
    add x3 -> x0, other arithmetic: 40 us -> none  [the longest x1 35.6 us: local(): residual + penalty[:, :, None] * chosen[None, None, :, None, None]]
    slice x15 -> x0, local copies, waits for them, and re-layouts: 33.8 us -> none  [the longest x5 19.2 us: pitch_derivative(): jnp.roll(along_pitch, reach, axis=4)]
    unnamed x2 -> x0, blocking collectives: 33.1 us -> none
    all_gather x1 -> x0, blocking collectives: 26.5 us -> none  [local(): whole = lax.all_gather(facing, 'pitch', axis=3, tiled=True)]
    pallas_call x0 -> x2, Pallas kernels: none -> 26.2 us  [the longest x1 24.2 us: local(): pl.pallas_call(functools.partial(exchange_kernel, count_p, count_r), out_...]
    unnamed x54 -> x10, local copies, waits for them, and re-layouts: 19.5 us -> 3.39 us
    ppermute x5 -> x0, starting transfers between devices: 11.8 us -> none  [the longest x2 5.27 us: padded_2(): before = lax.ppermute(last, axis, up)]
    unnamed x5 -> x0, other arithmetic: 6.74 us -> none
  transfers between devices with their start and end apart: 5 -> 0, of which waited for: 0 -> 0; matrix products, arithmetic and copies ran while one was open for 32% -> 0% of each run, Pallas kernels for 0% -> 0%
where the time goes in v1:
time: 30.4 us; the launch traced here: 30.2 us
  Pallas kernels  26.2 us (86%)
  local copies, waits for them, and re-layouts  3.39 us (11%)
  between operations  0.66 us (2%)
    pallas_call x1, Pallas kernels, local(): pl.pallas_call(functools.partial(exchange_kernel, count_p, count_r), out_...  24.2 us
    unnamed x10, local copies, waits for them, and re-layouts  3.39 us
    pallas_call x1, Pallas kernels, local(): pl.pallas_call(functools.partial(finish_kernel, count_p), out_shape=(bloc...  1.92 us

profile of v1, /device:TPU:0, one launch (start us, length us, event | category | flops | bytes accessed | tf_op | source)
XLA Modules:
  0.0 30.2 jit_solution(5313602973246801606)
XLA Ops:
  0.6 0.0 copy-start
  0.6 0.9 %copy-done = f32[288,128]{1,0:T(8,128)S(1)} copy-done((f32[288,128]{1,0:T(8,128)S(1)}, f32[288,128]{1,0:T(8,128)}, u32[]{:S(2)}) %copy-start) | copy-done | bytes 147480
  1.5 0.0 copy-start.2
  1.5 1.0 %copy-done.2 = f32[9,4,2,8,128]{4,3,2,1,0:T(8,128)S(1)} copy-done((f32[9,4,2,8,128]{4,3,2,1,0:T(8,128)S(1)}, f32[9,4,2,8,128]{4,3,2,1,0:T(8,128)}, u32[]{:S(2)}) %copy-start.2) | copy-done | bytes 294936
  2.5 0.0 copy-start.3
  2.5 0.9 %copy-done.3 = f32[9,2,8,128]{3,2,1,0:T(8,128)S(1)} copy-done((f32[9,2,8,128]{3,2,1,0:T(8,128)S(1)}, f32[9,2,8,128]{3,2,1,0:T(8,128)}, u32[]{:S(2)}) %copy-start.3) | copy-done | bytes 73752
  3.4 0.0 copy-start.1
  3.4 24.2 %exchange.1 = (f32[9,5,2,8,128]{4,3,2,1,0:T(8,128)S(1)}, f32[9,5,2,8,128]{4,3,2,1,0:T(8,128)S(1)}, f32[4,9,5,8,128]{4,3,2,1,0:T(8,128)S(1)}) custom-call(f32[9,2,8,128]{3,2,1,0:T(8,128)S(1)} %copy-done.3, f32[9,4,2,8,128]{4,3,2,1,0:T(8,128)S(1)} %copy-done.2, f32[288,128]{1,0:T(8,128)S(1)} %copy-done), custom_call_target="tpu_custom_call" | custom-call | tf_op jit(solution)/shard_map/exchange/pallas_call | solution.py:403
  27.6 0.0 copy-start.4
  27.7 0.0 copy-done.1
  27.7 0.6 %copy-done.4 = s32[9]{0:T(128)S(1)} copy-done((s32[9]{0:T(128)S(1)}, s32[9]{0:T(128)}, u32[]{:S(2)}) %copy-start.4) | copy-done | bytes 60
  28.3 1.9 %finish.1 = (f32[9,5,2,8,128]{4,3,2,1,0:T(8,128)}, f32[9,5,2,8,128]{4,3,2,1,0:T(8,128)}) custom-call(s32[9]{0:T(128)S(1)} %copy-done.4, f32[288,128]{1,0:T(8,128)S(1)} %copy-done.1, f32[4,9,5,8,128]{4,3,2,1,0:T(8,128)S(1)} %get-tuple-element.5.whole, f32[9,5,2,8,128]{4,3,2,1,0:T(8,128)S(1)} %get-tuple-element.6.base, ...), custom_call_target="tpu_custom_call" | custom-call | tf_op jit(solution)/shard_map/finish/pallas_call | solution.py:435
Async XLA Ops:
  0.6 0.9 %copy-start = (f32[288,128]{1,0:T(8,128)S(1)}, f32[288,128]{1,0:T(8,128)}, u32[]{:S(2)}) copy-start(f32[288,128]{1,0:T(8,128)} %constant.2.clone.table) | copy-start | bytes 442372
  1.5 1.0 %copy-start.2 = (f32[9,4,2,8,128]{4,3,2,1,0:T(8,128)S(1)}, f32[9,4,2,8,128]{4,3,2,1,0:T(8,128)}, u32[]{:S(2)}) copy-start(f32[9,4,2,8,128]{4,3,2,1,0:T(8,128)} %moments.1) | copy-start | bytes 884740
  2.5 0.9 %copy-start.3 = (f32[9,2,8,128]{3,2,1,0:T(8,128)S(1)}, f32[9,2,8,128]{3,2,1,0:T(8,128)}, u32[]{:S(2)}) copy-start(f32[9,2,8,128]{3,2,1,0:T(8,128)} %density.1) | copy-start | bytes 221188
  3.4 24.3 %copy-start.1 = (f32[288,128]{1,0:T(8,128)S(1)}, f32[288,128]{1,0:T(8,128)}, u32[]{:S(2)}) copy-start(f32[288,128]{1,0:T(8,128)} %constant.2.clone.table) | copy-start | bytes 442372
  27.6 0.7 %copy-start.4 = (s32[9]{0:T(128)S(1)}, s32[9]{0:T(128)}, u32[]{:S(2)}) copy-start(s32[9]{0:T(128)} %shifts.1) | copy-start | bytes 112

commit v2 on v1

v2 whole, which is shorter than its diff:
```python
import functools
import math

import jax
import jax.numpy as jnp
import numpy as np
from jax import lax
from jax.experimental import pallas as pl
from jax.experimental.pallas import tpu as pltpu
from jax.sharding import PartitionSpec as P

COEFFS = (0.75, -0.15, 1.0 / 60.0)
GAMMA_LESS = 0.4
HIGHEST = lax.Precision.HIGHEST
MESH = pl.DeviceIdType.MESH
VMEM = pl.BlockSpec(memory_space=pltpu.VMEM)
HBM = pl.BlockSpec(memory_space=pltpu.HBM)


def filter_constants(extent):
    eps = float(extent * extent // 16)
    decay = 2.0 * eps / (1.0 + 2.0 * eps + math.sqrt(1.0 + 4.0 * eps))
    gain = 1.0 / (math.sqrt(1.0 + 4.0 * eps) * (1.0 - decay**extent))
    return decay, gain


def tables(width, extent):
    decay, gain = filter_constants(extent)
    points = np.arange(width)
    apart = np.abs(points[:, None] - points[None, :])
    green = gain * (decay**apart + decay ** (extent - apart))
    deriv = np.zeros((width, width))
    rims = np.zeros((8, width))
    picks = np.zeros((8, width))
    for offset, weight in enumerate(COEFFS):
        reach = offset + 1
        for i in range(width):
            if i + reach < width:
                deriv[i + reach, i] += weight
            else:
                rims[i + reach - width, i] += weight
            if i - reach >= 0:
                deriv[i - reach, i] -= weight
            else:
                rims[4 + i - reach + 3, i] -= weight
    for h in range(3):
        picks[h, h] = 1.0
        picks[4 + h, width - 3 + h] = 1.0
    sums = np.zeros((8, width))
    sums[0] = decay ** (width - 1.0 - points)
    sums[1] = decay ** (points + 0.0)
    spread = np.zeros((8, width))
    spread[0] = gain * decay ** (points + 1.0)
    spread[1] = gain * decay ** (width - points + 0.0)
    return np.concatenate([deriv, green, rims, picks, sums, spread]).astype(np.float32)


def dot(a, b):
    return jnp.dot(a, b, precision=HIGHEST, preferred_element_type=jnp.float32)


def dot_nt(a, b):
    return lax.dot_general(
        a, b, (((1,), (1,)), ((), ())), precision=HIGHEST, preferred_element_type=jnp.float32
    )


def dot_tn(a, b):
    return lax.dot_general(
        a, b, (((0,), (0,)), ((), ())), precision=HIGHEST, preferred_element_type=jnp.float32
    )


def exchange_kernel(
    count_p,
    count_r,
    shifts_hbm,
    density_hbm,
    moments_hbm,
    table_hbm,
    base,
    smoothed,
    landed,
    shifts,
    density,
    moments,
    table,
    plane_out,
    loop_in,
    lined_up,
    along_p,
    along_r,
    rim_out,
    rim_in,
    sum_out,
    sum_in,
    load_sem,
    cross_send,
    cross_recv,
    back_send,
    back_recv,
    rim_send,
    rim_recv,
    radial_send,
    radial_recv,
    sum_send,
    sum_recv,
):
    inst, planes, rad, width = density.shape
    rows = inst * 5 * planes * rad
    units = loop_in.shape[1]
    extent = width * count_p
    decay, _ = filter_constants(extent)
    p = lax.axis_index("pitch")
    r = lax.axis_index("radial")
    a = lax.axis_index("axial")
    plane = (planes - 1) * (1 - a)

    loads = [
        pltpu.make_async_copy(src, dst, load_sem.at[i])
        for i, (src, dst) in enumerate(
            (
                (density_hbm, density),
                (moments_hbm, moments),
                (table_hbm, table),
                (shifts_hbm, shifts),
            )
        )
    ]
    for load in loads:
        load.start()

    barrier = pltpu.get_barrier_semaphore()
    for k in range(count_p):
        where = lax.rem(p + k, count_p)
        if k > 0:
            pl.semaphore_signal(barrier, inc=1, device_id=(where, r, a), device_id_type=MESH)
        pl.semaphore_signal(barrier, inc=1, device_id=(where, r, 1 - a), device_id_type=MESH)
    for k in (1, count_r - 1):
        pl.semaphore_signal(
            barrier, inc=1, device_id=(p, lax.rem(r + k, count_r), a), device_id_type=MESH
        )

    loads[0].wait()
    loads[1].wait()
    for n in range(inst):
        plane_out[5 * n] = density[n, plane]
        for v in range(4):
            plane_out[5 * n + 1 + v] = moments[n, v, plane]
    if count_p * units > 5 * inst:
        spare = count_p * units - 5 * inst
        plane_out[5 * inst :] = jnp.zeros((spare, rad, width), jnp.float32)

    pl.semaphore_wait(barrier, 2 * count_p + 1)

    def cross(k):
        where = lax.rem(p + k, count_p)
        return pltpu.make_async_remote_copy(
            src_ref=plane_out.at[pl.ds(where * units, units)],
            dst_ref=loop_in.at[p],
            send_sem=cross_send.at[k],
            recv_sem=cross_recv.at[k],
            device_id=(where, r, 1 - a),
            device_id_type=MESH,
        )

    def crossed(k):
        source = lax.rem(p + count_p - k, count_p)
        return pltpu.make_async_remote_copy(
            src_ref=plane_out.at[0:units],
            dst_ref=loop_in.at[source],
            send_sem=cross_send.at[k],
            recv_sem=cross_recv.at[k],
            device_id=(source, r, 1 - a),
            device_id_type=MESH,
        )

    order = sorted(range(count_p), key=lambda k: -min(k, count_p - k))
    for k in order:
        cross(k).start()

    rho = density[...]
    axial_m, radial_m, pitch_m, energy = (moments[:, v] for v in range(4))
    inverse = 1.0 / rho
    pressure = GAMMA_LESS * (
        energy - 0.5 * (axial_m * axial_m + radial_m * radial_m + pitch_m * pitch_m) * inverse
    )
    pitch_v = pitch_m * inverse
    radial_v = radial_m * inverse
    enthalpy = energy + pressure
    along_p[:, 0] = pitch_m
    along_p[:, 1] = axial_m * pitch_v
    along_p[:, 2] = radial_m * pitch_v
    along_p[:, 3] = pitch_m * pitch_v + pressure
    along_p[:, 4] = enthalpy * pitch_v
    mine = slice(rad, 2 * rad)
    along_r[:, 0, :, mine] = radial_m
    along_r[:, 1, :, mine] = axial_m * radial_v
    along_r[:, 2, :, mine] = radial_m * radial_v + pressure
    along_r[:, 3, :, mine] = pitch_m * radial_v
    along_r[:, 4, :, mine] = enthalpy * radial_v

    @pl.when(r == 0)
    def _():
        along_r[:, :, :, 0:rad] = jnp.zeros((inst, 5, planes, rad, width), jnp.float32)

    @pl.when(r == count_r - 1)
    def _():
        along_r[:, :, :, 2 * rad : 3 * rad] = jnp.zeros(
            (inst, 5, planes, rad, width), jnp.float32
        )

    def radial_copy(up):
        if up:
            src = along_r.at[:, :, :, 2 * rad - 3 : 2 * rad]
            dst = along_r.at[:, :, :, rad - 3 : rad]
            target = r + 1
        else:
            src = along_r.at[:, :, :, rad : rad + 3]
            dst = along_r.at[:, :, :, 2 * rad : 2 * rad + 3]
            target = r - 1
        return pltpu.make_async_remote_copy(
            src_ref=src,
            dst_ref=dst,
            send_sem=radial_send.at[int(up)],
            recv_sem=radial_recv.at[int(up)],
            device_id=(p, target, a),
            device_id_type=MESH,
        )

    pl.when(r < count_r - 1)(lambda: radial_copy(True).start())
    pl.when(r > 0)(lambda: radial_copy(False).start())

    loads[2].wait()
    loads[3].wait()
    flat_p = along_p[...].reshape(rows, width)
    rim_out[...] = dot_nt(table[2 * width + 8 : 2 * width + 16], flat_p)

    def rim_copy(up):
        part = slice(4, 8) if up else slice(0, 4)
        return pltpu.make_async_remote_copy(
            src_ref=rim_out.at[part],
            dst_ref=rim_in.at[part],
            send_sem=rim_send.at[int(up)],
            recv_sem=rim_recv.at[int(up)],
            device_id=(lax.rem(p + (1 if up else count_p - 1), count_p), r, a),
            device_id_type=MESH,
        )

    rim_copy(True).start()
    rim_copy(False).start()

    base[...] = dot(flat_p, table[0:width]).reshape(inst, 5, planes, rad, width)
    for v, field in enumerate((rho, axial_m, radial_m, pitch_m, energy)):
        total = None
        for k in range(1, (inst + 1) // 2):
            weight = 0.5 * (-1.0) ** k / math.sin(math.pi * k / inst)
            back = jnp.concatenate([field[inst - k :], field[: inst - k]], axis=0)
            ahead = jnp.concatenate([field[k:], field[:k]], axis=0)
            term = weight * (back - ahead)
            total = term if total is None else total + term
        for b in range(planes):
            on = jnp.where(plane == b, 1.0, 0.0).astype(jnp.float32)
            base[:, v, b] += total[:, b] - on * field[:, b]

    for k in order[::-1]:
        crossed(k).wait_recv()
    lane = lax.broadcasted_iota(jnp.int32, (rad, width), 1)
    for u in range(units):
        n = lax.min(lax.div(p * units + u, 5), inst - 1)
        shift = shifts[n]
        start = lax.rem(jnp.where(a == 1, extent - shift, shift), extent)
        block = lax.div(start, width)
        inside = start - block * width
        turn = lax.rem(width - inside, width)
        parts = [loop_in[lax.rem(block + b, count_p), u] for b in range(count_p)]
        for b in range(count_p):
            merged = jnp.where(lane >= inside, parts[b], parts[(b + 1) % count_p])
            lined_up[b, u] = pltpu.roll(merged, turn, 1)
    held = units * rad
    sums = [
        dot_nt(
            table[2 * width + 16 : 2 * width + 24],
            lined_up[b, 0:units].reshape(held, width),
        )
        for b in range(count_p)
    ]
    for b in range(count_p):
        ahead = None
        behind = None
        for k in range(1, count_p):
            other = sums[(b - k) % count_p]
            left = decay ** (width * (k - 1.0)) * other[0:1]
            right = decay ** (width * (count_p - k - 1.0)) * other[1:2]
            ahead = left if ahead is None else ahead + left
            behind = right if behind is None else behind + right
        carried = jnp.concatenate([ahead, behind, jnp.zeros((6, held), jnp.float32)], axis=0)
        if held < width:
            carried = jnp.concatenate(
                [carried, jnp.zeros((8, width - held), jnp.float32)], axis=1
            )
        lined_up[b, units] = carried

    def back(k):
        where = lax.rem(p + k, count_p)
        return pltpu.make_async_remote_copy(
            src_ref=lined_up.at[where],
            dst_ref=landed.at[p],
            send_sem=back_send.at[k - 1],
            recv_sem=back_recv.at[k - 1],
            device_id=(where, r, a),
            device_id_type=MESH,
        )

    def landing(k):
        source = lax.rem(p + count_p - k, count_p)
        return pltpu.make_async_remote_copy(
            src_ref=lined_up.at[source],
            dst_ref=landed.at[source],
            send_sem=back_send.at[k - 1],
            recv_sem=back_recv.at[k - 1],
            device_id=(source, r, a),
            device_id_type=MESH,
        )

    for k in order:
        if k > 0:
            back(k).start()
    landed[p] = lined_up[p]

    pl.when(r > 0)(lambda: radial_copy(True).wait_recv())
    pl.when(r < count_r - 1)(lambda: radial_copy(False).wait_recv())
    rim_copy(True).wait_recv()
    rim_copy(False).wait_recv()
    across = dot_tn(rim_in[...], table[2 * width : 2 * width + 8])
    radial = None
    for offset, weight in enumerate(COEFFS):
        k = offset + 1
        term = weight * (
            along_r[:, :, :, rad + k : 2 * rad + k] - along_r[:, :, :, rad - k : 2 * rad - k]
        )
        radial = term if radial is None else radial + term
    base[...] += across.reshape(inst, 5, planes, rad, width) + radial
    flat = base[...].reshape(rows, width)
    sum_out[...] = dot_nt(table[2 * width + 16 : 2 * width + 24], flat)

    def sum_copy(k):
        return pltpu.make_async_remote_copy(
            src_ref=sum_out.at[0:2],
            dst_ref=sum_in.at[k - 1],
            send_sem=sum_send.at[k - 1],
            recv_sem=sum_recv.at[k - 1],
            device_id=(lax.rem(p + k, count_p), r, a),
            device_id_type=MESH,
        )

    for k in range(1, count_p):
        sum_copy(k).start()
    smoothed[...] = dot(flat, table[width : 2 * width]).reshape(inst, 5, planes, rad, width)
    ahead = None
    behind = None
    for k in range(1, count_p):
        sum_copy(k).wait_recv()
        left = decay ** (width * (k - 1.0)) * sum_in[k - 1, 0:1]
        right = decay ** (width * (count_p - k - 1.0)) * sum_in[k - 1, 1:2]
        ahead = left if ahead is None else ahead + left
        behind = right if behind is None else behind + right
    carried = jnp.concatenate([ahead, behind, jnp.zeros((6, rows), jnp.float32)], axis=0)
    smoothed[...] += dot_tn(carried, table[2 * width + 24 : 2 * width + 32]).reshape(
        inst, 5, planes, rad, width
    )

    for k in range(1, count_p):
        landing(k).wait_recv()
        back(k).wait_send()
        sum_copy(k).wait_send()
    for k in range(count_p):
        cross(k).wait_send()
    pl.when(r < count_r - 1)(lambda: radial_copy(True).wait_send())
    pl.when(r > 0)(lambda: radial_copy(False).wait_send())
    rim_copy(True).wait_send()
    rim_copy(False).wait_send()


def finish_kernel(count_p, table, landed, base, smoothed, residual, update):
    inst, _, planes, rad, width = base.shape
    units = landed.shape[1] - 1
    held = units * rad
    a = lax.axis_index("axial")
    plane = (planes - 1) * (1 - a)
    spread = table[2 * width + 24 : 2 * width + 32]
    residual[...] = base[...]
    update[...] = smoothed[...]
    for i in range(count_p):
        share = landed[i, 0:units].reshape(held, width)
        filtered = dot(share, table[width : 2 * width]) + dot_tn(landed[i, units], spread)[:held]
        for u in range(units):
            unit = i * units + u
            if unit < 5 * inst:
                n, v = divmod(unit, 5)
                residual[n, v, plane] += share[u * rad : (u + 1) * rad]
                update[n, v, plane] += filtered[u * rad : (u + 1) * rad]


def local(density, moments, shifts):
    count_p = lax.axis_size("pitch")
    count_r = lax.axis_size("radial")
    inst, planes, rad, width = density.shape
    rows = inst * 5 * planes * rad
    units = -(-5 * inst // count_p)
    table = jnp.asarray(tables(width, width * count_p))
    block = jax.ShapeDtypeStruct((inst, 5, planes, rad, width), jnp.float32)
    dma = pltpu.SemaphoreType.DMA
    base, smoothed, landed = pl.pallas_call(
        functools.partial(exchange_kernel, count_p, count_r),
        out_shape=(
            block,
            block,
            jax.ShapeDtypeStruct((count_p, units + 1, rad, width), jnp.float32),
        ),
        in_specs=[HBM] * 4,
        out_specs=(VMEM,) * 3,
        scratch_shapes=[
            pltpu.SMEM((inst,), jnp.int32),
            pltpu.VMEM(density.shape, jnp.float32),
            pltpu.VMEM(moments.shape, jnp.float32),
            pltpu.VMEM(table.shape, jnp.float32),
            pltpu.VMEM((count_p * units, rad, width), jnp.float32),
            pltpu.VMEM((count_p, units, rad, width), jnp.float32),
            pltpu.VMEM((count_p, units + 1, rad, width), jnp.float32),
            pltpu.VMEM((inst, 5, planes, rad, width), jnp.float32),
            pltpu.VMEM((inst, 5, planes, 3 * rad, width), jnp.float32),
            pltpu.VMEM((8, rows), jnp.float32),
            pltpu.VMEM((8, rows), jnp.float32),
            pltpu.VMEM((8, rows), jnp.float32),
            pltpu.VMEM((count_p - 1, 2, rows), jnp.float32),
            dma((4,)),
            dma((count_p,)),
            dma((count_p,)),
            dma((count_p - 1,)),
            dma((count_p - 1,)),
            dma((2,)),
            dma((2,)),
            dma((2,)),
            dma((2,)),
            dma((count_p - 1,)),
            dma((count_p - 1,)),
        ],
        compiler_params=pltpu.CompilerParams(
            collective_id=0, has_side_effects=True, vmem_limit_bytes=40 * 2**20
        ),
        name="exchange",
    )(shifts, density, moments, table)
    return pl.pallas_call(
        functools.partial(finish_kernel, count_p),
        out_shape=(block, block),
        in_specs=[VMEM] * 4,
        out_specs=(VMEM,) * 2,
        compiler_params=pltpu.CompilerParams(vmem_limit_bytes=40 * 2**20),
        name="finish",
    )(table, landed, base, smoothed)


def solution(mesh):
    in_specs = (P(None, "axial", "radial", "pitch"), P(None, None, "axial", "radial", "pitch"), P())
    out_specs = (
        P(None, None, "axial", "radial", "pitch"),
        P(None, None, "axial", "radial", "pitch"),
    )
    return jax.shard_map(local, mesh=mesh, in_specs=in_specs, out_specs=out_specs, check_vma=False)
```

time: 30.4 us -> 26.4 us (0.87)
  Pallas kernels: 26.2 us -> 22.1 us
    pallas_call x1, Pallas kernels: 24.2 us -> 20.6 us  [local(): pl.pallas_call(functools.partial(exchange_kernel, count_p, count_r), out_...]
    pallas_call x1, Pallas kernels: 1.92 us -> 1.46 us  [local(): pl.pallas_call(functools.partial(finish_kernel, count_p), out_shape=(bloc...]
where the time goes in v2:
time: 26.4 us; the launch traced here: 26.1 us
  Pallas kernels  22.1 us (84%)
  local copies, waits for them, and re-layouts  3.41 us (13%)
  between operations  0.66 us (2%)
    pallas_call x1, Pallas kernels, local(): pl.pallas_call(functools.partial(exchange_kernel, count_p, count_r), out_...  20.6 us
    unnamed x10, local copies, waits for them, and re-layouts  3.41 us
    pallas_call x1, Pallas kernels, local(): pl.pallas_call(functools.partial(finish_kernel, count_p), out_shape=(bloc...  1.46 us

profile of v2, /device:TPU:0, one launch (start us, length us, event | category | flops | bytes accessed | tf_op | source)
XLA Modules:
  0.0 26.1 jit_solution(545800832190969087)
XLA Ops:
  0.6 0.0 copy-start
  0.6 0.9 %copy-done = f32[288,128]{1,0:T(8,128)S(1)} copy-done((f32[288,128]{1,0:T(8,128)S(1)}, f32[288,128]{1,0:T(8,128)}, u32[]{:S(2)}) %copy-start) | copy-done | bytes 147480
  1.5 0.0 copy-start.2
  1.5 1.0 %copy-done.2 = f32[9,4,2,8,128]{4,3,2,1,0:T(8,128)S(1)} copy-done((f32[9,4,2,8,128]{4,3,2,1,0:T(8,128)S(1)}, f32[9,4,2,8,128]{4,3,2,1,0:T(8,128)}, u32[]{:S(2)}) %copy-start.2) | copy-done | bytes 294936
  2.5 0.0 copy-start.3
  2.5 0.9 %copy-done.3 = f32[9,2,8,128]{3,2,1,0:T(8,128)S(1)} copy-done((f32[9,2,8,128]{3,2,1,0:T(8,128)S(1)}, f32[9,2,8,128]{3,2,1,0:T(8,128)}, u32[]{:S(2)}) %copy-start.3) | copy-done | bytes 73752
  3.4 0.0 copy-start.4
  3.4 0.7 %copy-done.4 = s32[9]{0:T(128)S(1)} copy-done((s32[9]{0:T(128)S(1)}, s32[9]{0:T(128)}, u32[]{:S(2)}) %copy-start.4) | copy-done | bytes 60
  4.0 0.0 copy-start.1
  4.0 20.6 %exchange.1 = (f32[9,5,2,8,128]{4,3,2,1,0:T(8,128)S(1)}, f32[9,5,2,8,128]{4,3,2,1,0:T(8,128)S(1)}, f32[4,13,8,128]{3,2,1,0:T(8,128)S(1)}) custom-call(s32[9]{0:T(128)S(1)} %copy-done.4, f32[9,2,8,128]{3,2,1,0:T(8,128)S(1)} %copy-done.3, f32[9,4,2,8,128]{4,3,2,1,0:T(8,128)S(1)} %copy-done.2, f32[288,128]{1,0:T(8,128)S(1)} %copy-done), custom_call_target="tpu_custom_call" | custom-call | tf_op jit(solution)/shard_map/exchange/pallas_call | solution.py:414
  24.7 0.0 copy-done.1
  24.7 1.5 %finish.1 = (f32[9,5,2,8,128]{4,3,2,1,0:T(8,128)}, f32[9,5,2,8,128]{4,3,2,1,0:T(8,128)}) custom-call(f32[288,128]{1,0:T(8,128)S(1)} %copy-done.1, f32[4,13,8,128]{3,2,1,0:T(8,128)S(1)} %get-tuple-element.5.landed, f32[9,5,2,8,128]{4,3,2,1,0:T(8,128)S(1)} %get-tuple-element.6.base, f32[9,5,2,8,128]{4,3,2,1,0:T(8,128)S(1)} %get-tuple-element.7.smoothed), custom_call_target="tpu_custom_call" | custom-call | tf_op jit(solution)/shard_map/finish/pallas_call | solution.py:454
Async XLA Ops:
  0.6 0.9 %copy-start = (f32[288,128]{1,0:T(8,128)S(1)}, f32[288,128]{1,0:T(8,128)}, u32[]{:S(2)}) copy-start(f32[288,128]{1,0:T(8,128)} %constant.2.clone.table_hbm.table) | copy-start | bytes 442372
  1.5 1.0 %copy-start.2 = (f32[9,4,2,8,128]{4,3,2,1,0:T(8,128)S(1)}, f32[9,4,2,8,128]{4,3,2,1,0:T(8,128)}, u32[]{:S(2)}) copy-start(f32[9,4,2,8,128]{4,3,2,1,0:T(8,128)} %moments_hbm.1) | copy-start | bytes 884740
  2.5 0.9 %copy-start.3 = (f32[9,2,8,128]{3,2,1,0:T(8,128)S(1)}, f32[9,2,8,128]{3,2,1,0:T(8,128)}, u32[]{:S(2)}) copy-start(f32[9,2,8,128]{3,2,1,0:T(8,128)} %density_hbm.1) | copy-start | bytes 221188
  3.4 0.7 %copy-start.4 = (s32[9]{0:T(128)S(1)}, s32[9]{0:T(128)}, u32[]{:S(2)}) copy-start(s32[9]{0:T(128)} %shifts_hbm.1) | copy-start | bytes 112
  4.0 20.6 %copy-start.1 = (f32[288,128]{1,0:T(8,128)S(1)}, f32[288,128]{1,0:T(8,128)}, u32[]{:S(2)}) copy-start(f32[288,128]{1,0:T(8,128)} %constant.2.clone.table_hbm.table) | copy-start | bytes 442372

commit v3 on v2

--- a/solution.py
+++ b/solution.py
@@ -13,7 +13,7 @@
 GAMMA_LESS = 0.4
 HIGHEST = lax.Precision.HIGHEST
 MESH = pl.DeviceIdType.MESH
-VMEM = pl.BlockSpec(memory_space=pltpu.VMEM)
+VMEM_LIMIT = 60 * 2**20
 HBM = pl.BlockSpec(memory_space=pltpu.HBM)
 
 
@@ -78,9 +78,11 @@
     density_hbm,
     moments_hbm,
     table_hbm,
+    base_hbm,
+    smoothed_hbm,
+    landed,
     base,
     smoothed,
-    landed,
     shifts,
     density,
     moments,
@@ -95,6 +97,7 @@
     sum_out,
     sum_in,
     load_sem,
+    store_sem,
     cross_send,
     cross_recv,
     back_send,
@@ -263,6 +266,38 @@
             on = jnp.where(plane == b, 1.0, 0.0).astype(jnp.float32)
             base[:, v, b] += total[:, b] - on * field[:, b]
 
+    pl.when(r > 0)(lambda: radial_copy(True).wait_recv())
+    pl.when(r < count_r - 1)(lambda: radial_copy(False).wait_recv())
+    rim_copy(True).wait_recv()
+    rim_copy(False).wait_recv()
+    across = dot_tn(rim_in[...], table[2 * width : 2 * width + 8])
+    radial = None
+    for offset, weight in enumerate(COEFFS):
+        k = offset + 1
+        term = weight * (
+            along_r[:, :, :, rad + k : 2 * rad + k] - along_r[:, :, :, rad - k : 2 * rad - k]
+        )
+        radial = term if radial is None else radial + term
+    base[...] += across.reshape(inst, 5, planes, rad, width) + radial
+    flat = base[...].reshape(rows, width)
+    sum_out[...] = dot_nt(table[2 * width + 16 : 2 * width + 24], flat)
+
+    def sum_copy(k):
+        return pltpu.make_async_remote_copy(
+            src_ref=sum_out.at[0:2],
+            dst_ref=sum_in.at[k - 1],
+            send_sem=sum_send.at[k - 1],
+            recv_sem=sum_recv.at[k - 1],
+            device_id=(lax.rem(p + k, count_p), r, a),
+            device_id_type=MESH,
+        )
+
+    for k in range(1, count_p):
+        sum_copy(k).start()
+    store_base = pltpu.make_async_copy(base, base_hbm, store_sem.at[0])
+    store_base.start()
+    smoothed[...] = dot(flat, table[width : 2 * width]).reshape(inst, 5, planes, rad, width)
+
     for k in order[::-1]:
         crossed(k).wait_recv()
     lane = lax.broadcasted_iota(jnp.int32, (rad, width), 1)
@@ -326,37 +361,9 @@
     for k in order:
         if k > 0:
             back(k).start()
-    landed[p] = lined_up[p]
-
-    pl.when(r > 0)(lambda: radial_copy(True).wait_recv())
-    pl.when(r < count_r - 1)(lambda: radial_copy(False).wait_recv())
-    rim_copy(True).wait_recv()
-    rim_copy(False).wait_recv()
-    across = dot_tn(rim_in[...], table[2 * width : 2 * width + 8])
-    radial = None
-    for offset, weight in enumerate(COEFFS):
-        k = offset + 1
-        term = weight * (
-            along_r[:, :, :, rad + k : 2 * rad + k] - along_r[:, :, :, rad - k : 2 * rad - k]
-        )
-        radial = term if radial is None else radial + term
-    base[...] += across.reshape(inst, 5, planes, rad, width) + radial
-    flat = base[...].reshape(rows, width)
-    sum_out[...] = dot_nt(table[2 * width + 16 : 2 * width + 24], flat)
-
-    def sum_copy(k):
-        return pltpu.make_async_remote_copy(
-            src_ref=sum_out.at[0:2],
-            dst_ref=sum_in.at[k - 1],
-            send_sem=sum_send.at[k - 1],
-            recv_sem=sum_recv.at[k - 1],
-            device_id=(lax.rem(p + k, count_p), r, a),
-            device_id_type=MESH,
-        )
-
-    for k in range(1, count_p):
-        sum_copy(k).start()
-    smoothed[...] = dot(flat, table[width : 2 * width]).reshape(inst, 5, planes, rad, width)
+    keep = pltpu.make_async_copy(lined_up.at[p], landed.at[p], store_sem.at[2])
+    keep.start()
+
     ahead = None
     behind = None
     for k in range(1, count_p):
@@ -370,6 +377,12 @@
         inst, 5, planes, rad, width
     )
 
+    store_smoothed = pltpu.make_async_copy(smoothed, smoothed_hbm, store_sem.at[1])
+    store_smoothed.start()
+
+    store_base.wait()
+    keep.wait()
+    store_smoothed.wait()
     for k in range(1, count_p):
         landing(k).wait_recv()
         back(k).wait_send()
@@ -382,15 +395,42 @@
     rim_copy(False).wait_send()
 
 
-def finish_kernel(count_p, table, landed, base, smoothed, residual, update):
-    inst, _, planes, rad, width = base.shape
+def finish_kernel(
+    count_p,
+    table_hbm,
+    landed_hbm,
+    base_hbm,
+    smoothed_hbm,
+    residual_hbm,
+    update_hbm,
+    table,
+    landed,
+    residual,
+    update,
+    load_sem,
+    store_sem,
+):
+    loads = [
+        pltpu.make_async_copy(src, dst, load_sem.at[i])
+        for i, (src, dst) in enumerate(
+            (
+                (table_hbm, table),
+                (landed_hbm, landed),
+                (smoothed_hbm, update),
+                (base_hbm, residual),
+            )
+        )
+    ]
+    for load in loads:
+        load.start()
+    inst, _, planes, rad, width = residual.shape
     units = landed.shape[1] - 1
     held = units * rad
     a = lax.axis_index("axial")
     plane = (planes - 1) * (1 - a)
+    for load in loads:
+        load.wait()
     spread = table[2 * width + 24 : 2 * width + 32]
-    residual[...] = base[...]
-    update[...] = smoothed[...]
     for i in range(count_p):
         share = landed[i, 0:units].reshape(held, width)
         filtered = dot(share, table[width : 2 * width]) + dot_tn(landed[i, units], spread)[:held]
@@ -400,6 +440,14 @@
                 n, v = divmod(unit, 5)
                 residual[n, v, plane] += share[u * rad : (u + 1) * rad]
                 update[n, v, plane] += filtered[u * rad : (u + 1) * rad]
+    stores = [
+        pltpu.make_async_copy(residual, residual_hbm, store_sem.at[0]),
+        pltpu.make_async_copy(update, update_hbm, store_sem.at[1]),
+    ]
+    for store in stores:
+        store.start()
+    for store in stores:
+        store.wait()
 
 
 def local(density, moments, shifts):
@@ -419,8 +467,10 @@
             jax.ShapeDtypeStruct((count_p, units + 1, rad, width), jnp.float32),
         ),
         in_specs=[HBM] * 4,
-        out_specs=(VMEM,) * 3,
+        out_specs=(HBM,) * 3,
         scratch_shapes=[
+            pltpu.VMEM(block.shape, jnp.float32),
+            pltpu.VMEM(block.shape, jnp.float32),
             pltpu.SMEM((inst,), jnp.int32),
             pltpu.VMEM(density.shape, jnp.float32),
             pltpu.VMEM(moments.shape, jnp.float32),
@@ -435,6 +485,7 @@
             pltpu.VMEM((8, rows), jnp.float32),
             pltpu.VMEM((count_p - 1, 2, rows), jnp.float32),
             dma((4,)),
+            dma((3,)),
             dma((count_p,)),
             dma((count_p,)),
             dma((count_p - 1,)),
@@ -447,16 +498,24 @@
             dma((count_p - 1,)),
         ],
         compiler_params=pltpu.CompilerParams(
-            collective_id=0, has_side_effects=True, vmem_limit_bytes=40 * 2**20
+            collective_id=0, has_side_effects=True, vmem_limit_bytes=VMEM_LIMIT
         ),
         name="exchange",
     )(shifts, density, moments, table)
     return pl.pallas_call(
         functools.partial(finish_kernel, count_p),
         out_shape=(block, block),
-        in_specs=[VMEM] * 4,
-        out_specs=(VMEM,) * 2,
-        compiler_params=pltpu.CompilerParams(vmem_limit_bytes=40 * 2**20),
+        in_specs=[HBM] * 4,
+        out_specs=(HBM,) * 2,
+        scratch_shapes=[
+            pltpu.VMEM(table.shape, jnp.float32),
+            pltpu.VMEM((count_p, units + 1, rad, width), jnp.float32),
+            pltpu.VMEM(block.shape, jnp.float32),
+            pltpu.VMEM(block.shape, jnp.float32),
+            dma((4,)),
+            dma((2,)),
+        ],
+        compiler_params=pltpu.CompilerParams(vmem_limit_bytes=VMEM_LIMIT),
         name="finish",
     )(table, landed, base, smoothed)
 

time: 26.4 us -> 23.9 us (0.905)
  local copies, waits for them, and re-layouts: 3.41 us -> 0 us
  Pallas kernels: 22.1 us -> 23.1 us
    unnamed x10 -> x0, local copies, waits for them, and re-layouts: 3.41 us -> none
    pallas_call x1, Pallas kernels: 1.46 us -> 2.71 us  [local(): pl.pallas_call(functools.partial(finish_kernel, count_p), out_shape=(bloc...]
    pallas_call x1, Pallas kernels: 20.6 us -> 20.3 us  [local(): pl.pallas_call(functools.partial(exchange_kernel, count_p, count_r), out_...]
where the time goes in v3:
time: 23.9 us; the launch traced here: 23.7 us
  Pallas kernels  23.1 us (97%)
  between operations  0.64 us (3%)
    pallas_call x1, Pallas kernels, local(): pl.pallas_call(functools.partial(exchange_kernel, count_p, count_r), out_...  20.3 us
    pallas_call x1, Pallas kernels, local(): pl.pallas_call(functools.partial(finish_kernel, count_p), out_shape=(bloc...  2.71 us

profile of v3, /device:TPU:0, one launch (start us, length us, event | category | flops | bytes accessed | tf_op | source)
XLA Modules:
  0.0 23.7 jit_solution(17911875139874501736)
XLA Ops:
  0.6 20.3 %exchange.1 = (f32[9,5,2,8,128]{4,3,2,1,0:T(8,128)}, f32[9,5,2,8,128]{4,3,2,1,0:T(8,128)}, f32[4,13,8,128]{3,2,1,0:T(8,128)}) custom-call(s32[9]{0:T(128)} %shifts_hbm.1, f32[9,2,8,128]{3,2,1,0:T(8,128)} %density_hbm.1, f32[9,4,2,8,128]{4,3,2,1,0:T(8,128)} %moments_hbm.1, f32[288,128]{1,0:T(8,128)} %constant.2.clone.table_hbm), custom_call_target="tpu_custom_call" | custom-call | tf_op jit(solution)/shard_map/exchange/pallas_call | solution.py:462
  21.0 2.7 %finish.1 = (f32[9,5,2,8,128]{4,3,2,1,0:T(8,128)}, f32[9,5,2,8,128]{4,3,2,1,0:T(8,128)}) custom-call(f32[288,128]{1,0:T(8,128)} %constant.2.clone.table_hbm, f32[4,13,8,128]{3,2,1,0:T(8,128)} %get-tuple-element.5.landed_hbm, f32[9,5,2,8,128]{4,3,2,1,0:T(8,128)} %get-tuple-element.6.base_hbm, f32[9,5,2,8,128]{4,3,2,1,0:T(8,128)} %get-tuple-element.7.smoothed_hbm), custom_call_target="tpu_custom_call" | custom-call | tf_op jit(solution)/shard_map/finish/pallas_call | solution.py:505
